TPU v7x, 256 devices: a whole 4x4x8 slice. The times are simulated.
256 devices in a mesh: dom: 64 (over x, z, core), sub: 4 (over y).
Axes of the slice: x: 4, y: 4, z: 8, core: 2. Of those that a mesh axis runs over, the one named last changes fastest.
Arguments:
- elastic: bfloat16 [9, 35, 262144], P(None, None, ('dom', 'sub')), may hold values from -6 to 6
- jacobian: float32 [3, 262144], P(None, ('dom', 'sub')), may hold values from 0.5 to 2
- star_mats: float32 [3, 9, 9], replicated, may hold values from -2 to 2
- stiffness: bfloat16 [3, 35, 35], replicated, may hold values from -1 to 1
- face_proj: bfloat16 [4, 15, 35], replicated, may hold values from -1 to 1
- face_lift: bfloat16 [4, 35, 15], replicated, may hold values from -1.5 to 1.5
- clusters: int32 [262144], P(('dom', 'sub')), may hold values from 0 to 2
- neighbours: int32 [4, 262144], P(None, ('dom', 'sub')), may hold values from 0 to 4607, as said below
- send_faces: int32 [2, 65536], P(None, ('dom', 'sub')), may hold values from 0 to 4095, as said below
- fault_faces: int32 [32768], P(('dom', 'sub')), may hold values from 0 to 4095, as said below
- fault_strength: float32 [32768], P(('dom', 'sub')), may hold values from 0.2 to 2
- seafloor_faces: int32 [131072], P(('dom', 'sub')), may hold values from 0 to 4095, as said below
- seafloor_slots: int32 [131072], P(('dom', 'sub')), may hold values from 0 to 1023, as said below
- arrival_cells: int32 [262144], P(('dom', 'sub')), may hold values from 0 to 256, as said below
- ocean_state: float32 [3, 15, 16384], P(None, None, 'dom'), may hold values from -6 to 6
- ocean_kernels: float32 [2, 15, 15], replicated, may hold values from -1.5 to 1.5
- shallow_mats: float32 [2, 3, 3], replicated, may hold values from -3.5 to 3.5
- edge_proj: float32 [3, 5, 15], replicated, may hold values from -1.5 to 1.5
- edge_lift: float32 [3, 15, 5], replicated, may hold values from -2.5 to 2.5
- ocean_send: int32 [2, 2048], P(None, 'dom'), may hold values from 0 to 767, as said below
- ocean_neighbours: int32 [3, 16384], P(None, 'dom'), may hold values from 0 to 831, as said below
Outputs:
- elastic_next: bfloat16 [9, 35, 262144], P(None, None, ('dom', 'sub'))
- ocean_next: float32 [3, 15, 16384], P(None, None, 'dom')
Inputs may be any that keep to these rules, and one draw needn't show every extreme that they name: `neighbours`: slot f * 1024 + e is face f of local element e; slot 4096 + j is the j-th trace from the block before, 4352 + j the j-th from the block after; every such received slot is named exactly once in every block. `send_faces`: local face slots; row 0 is sent to the block before, row 1 to the block after; the 512 entries of one block are distinct. `fault_faces`: local face slots, distinct in one block. `seafloor_faces`: local face slots, distinct in one block. `seafloor_slots`: distinct in one block, so at most 16 faces of a block go to one ocean block; in every block some ocean block gets exactly 16. `arrival_cells`: entry s * 16 + k of element block (d, u) is the local ocean cell of ocean block d for place k from element block (s, u); it is 256 exactly where no face arrives. `ocean_send`: local edge slots; row 0 is sent to the ocean block before, row 1 to the block after; the 64 entries of one block are distinct. `ocean_neighbours`: slot g * 256 + c is edge g of local cell c; slot 768 + j is the j-th trace from the ocean block before, 800 + j the j-th from the block after; every such received slot is named exactly once in every block.
All inputs are finite; a program needn't handle non-finite values.
Results may differ from a plain program's by a relative error of at most 0.01.
Values may be sent and summed in bfloat16 or wider, within the bound.
A program may use at most 128 MiB of HBM per device.

v0:
```python
import functools

import jax
import jax.numpy as jnp
from jax import lax
from jax.experimental import pallas as pl
from jax.experimental.pallas import tpu as pltpu
from jax.sharding import PartitionSpec as P

MESH = pl.DeviceIdType.MESH
F32, BF16 = jnp.float32, jnp.bfloat16
HIGHEST = lax.Precision.HIGHEST

NV, NB, NF = 9, 35, 15
NO, NE = 3, 5
ROWS = 320
E = 1024
BF = 256
OC, OBF = 256, 32
CAP = 16
N_DOM, N_SUB = 64, 4
CHUNK = 256
ROOT3 = 0.57735027
ROOT2 = 0.70710678
TET = [
    [(2, -1.0)],
    [(1, -1.0)],
    [(0, -1.0)],
    [(0, ROOT3), (1, ROOT3), (2, ROOT3)],
]
TRI = [[(1, -1.0)], [(0, -1.0)], [(0, ROOT2), (1, ROOT2)]]


def iota(shape, dim):
    return lax.broadcasted_iota(jnp.int32, shape, dim)


def div35(x):
    return lax.shift_right_logical(x * 1873, 16)


def div15(x):
    return lax.shift_right_logical(x * 4370, 16)


def div5(x):
    return lax.shift_right_logical(x * 13108, 16)


def onehot(cond, dtype=BF16):
    return jnp.where(cond, 1.0, 0.0).astype(dtype)


def dot(a, b, precision=None):
    return lax.dot_general(
        a, b, (((1,), (0,)), ((), ())), precision=precision, preferred_element_type=F32
    )


def dot_tn(a, b, precision=None):
    return lax.dot_general(
        a, b, (((0,), (0,)), ((), ())), precision=precision, preferred_element_type=F32
    )


def dot_nt(a, b, precision=None):
    return lax.dot_general(
        a, b, (((1,), (1,)), ((), ())), precision=precision, preferred_element_type=F32
    )


def split(x):
    high = x.astype(BF16)
    return high, (x - high.astype(F32)).astype(BF16)


def combine(mats, pairs):
    total = None
    for direction, factor in pairs:
        term = mats[direction] * factor
        total = term if total is None else total + term
    return total


def spread(select_rows, mat, select_cols):
    high, low = split(mat)
    high = dot(high, select_cols).astype(BF16)
    low = dot(low, select_cols).astype(BF16)
    return dot(select_rows, high) + dot(select_rows, low)


def kernel(
    elastic,
    jac,
    star,
    stiff,
    fproj,
    flift,
    clusters,
    nbr_s,
    send_s,
    fault,
    strength,
    floor_s,
    slots,
    arrival,
    ocean,
    okern,
    shal,
    eproj,
    elift,
    osend_s,
    onbr_s,
    out_e,
    out_o,
    xf,
    xs,
    wmat,
    fmat,
    mmat,
    ext,
    beside,
    jm,
    accf,
    stage,
    fsend,
    frecv,
    oext,
    obeside,
    osend,
    orecv,
    ost,
    oacc,
    upl,
    pack,
    asend,
    arecv,
    part,
    fsend_sem,
    frecv_sem,
    osend_sem,
    orecv_sem,
    asend_sem,
    arecv_sem,
    psend_sem,
    precv_sem,
):
    dom = lax.axis_index("dom")
    sub = lax.axis_index("sub")
    block = dom * N_SUB + sub
    n_blocks = N_DOM * N_SUB
    after = lax.rem(block + 1, n_blocks)
    before = lax.rem(block + n_blocks - 1, n_blocks)
    after_id = (lax.div(after, N_SUB), lax.rem(after, N_SUB))
    before_id = (lax.div(before, N_SUB), lax.rem(before, N_SUB))
    dom_after = lax.rem(dom + 1, N_DOM)
    dom_before = lax.rem(dom + N_DOM - 1, N_DOM)

    barrier = pltpu.get_barrier_semaphore()

    def greet(k, carry):
        there = (lax.rem(dom + k, N_DOM), sub)
        pl.semaphore_signal(barrier, inc=1, device_id=there, device_id_type=MESH)
        return carry

    lax.fori_loop(1, N_DOM, greet, 0)
    for k in range(1, N_SUB):
        there = (dom, lax.rem(sub + k, N_SUB))
        pl.semaphore_signal(barrier, inc=1, device_id=there, device_id_type=MESH)
    for there in (before_id, after_id):
        pl.semaphore_signal(barrier, inc=1, device_id=there, device_id_type=MESH)

    row = iota((ROWS, 1), 0)
    row_v = div35(row)
    row_b = row - NB * row_v
    pick_v = onehot(row_v == iota((ROWS, NV), 1))
    pick_b = onehot(row_b == iota((ROWS, NB), 1))

    col = iota((1, 3 * ROWS), 1)
    col_d = (col >= ROWS).astype(jnp.int32) + (col >= 2 * ROWS).astype(jnp.int32)
    col_r = col - ROWS * col_d
    col_u = div35(col_r)
    col_c = col_r - NB * col_u
    a_high, a_low, k_cols = None, None, None
    for d in range(3):
        sel_u = onehot((col_d == d) & (col_u == iota((NV, 3 * ROWS), 0)))
        sel_c = onehot((col_d == d) & (col_c == iota((NB, 3 * ROWS), 0)))
        high, low = split(star[d])
        terms = (dot(high, sel_u), dot(low, sel_u), dot(stiff[d], sel_c))
        if d == 0:
            a_high, a_low, k_cols = terms
        else:
            a_high, a_low, k_cols = (
                a_high + terms[0],
                a_low + terms[1],
                k_cols + terms[2],
            )
    a_high, a_low, k_cols = a_high.astype(BF16), a_low.astype(BF16), k_cols.astype(BF16)
    wmat[:, : 3 * ROWS] = (
        (dot(pick_v, a_high) + dot(pick_v, a_low)) * dot(pick_b, k_cols)
    ).astype(BF16)

    q = iota((1, 256), 1)
    q_g = div15(q)
    q_u = jnp.where(q_g == 0, NV - 1, q_g - 1)
    q_j = q - NF * q_g
    q_ok = q_g < NV
    sel_j = onehot((q_j == iota((NF, 256), 0)) & q_ok)
    same_var = (row_v == q_u) & q_ok
    for f in range(4):
        proj = dot_tn(fproj[f], sel_j).astype(BF16)
        fmat[:, f * 256 : (f + 1) * 256] = jnp.where(
            same_var, dot(pick_b, proj), 0.0
        ).astype(BF16)

    for v in range(NV):
        xf[NB * v : NB * (v + 1), :] = elastic[v].astype(F32)
    xf[NV * NB :, :] = jnp.zeros((ROWS - NV * NB, E), F32)

    step = 0.5 * jnp.exp2(-clusters[...].astype(F32))
    for c in range(E // CHUNK):
        cols = slice(c * CHUNK, (c + 1) * CHUNK)

        def scaled(x):
            for d in range(3):
                xs[d * ROWS : (d + 1) * ROWS, cols] = (jac[d : d + 1, cols] * x).astype(
                    BF16
                )

        h = step[:, cols]
        x = xf[:, cols]
        scaled(x)
        term = dot(wmat[:, : 3 * ROWS], xs[: 3 * ROWS, cols])
        integral = h * x + (h * h * 0.5) * term
        scaled(term)
        term = dot(wmat[:, : 3 * ROWS], xs[: 3 * ROWS, cols])
        integral = (integral + (h * h * h * (1.0 / 6.0)) * term).astype(BF16)
        xs[3 * ROWS :, cols] = integral
        scaled(integral.astype(F32))
        traced = dot_tn(integral, fmat[...])
        for f in range(4):
            for half in range(2):
                lanes = slice((2 * f + half) * 128, (2 * f + half + 1) * 128)
                ext[half, f * E + c * CHUNK : f * E + (c + 1) * CHUNK, :] = traced[:, lanes]

    def gather_send(i, carry):
        for k in range(8):
            j = i * 8 + k
            for side in range(2):
                slot = send_s[side, j]
                for half in range(2):
                    stage[side, half, pl.ds(j, 1), :] = ext[half, pl.ds(slot, 1), :]
            for part_ in range(2):
                m = part_ * 256 + j
                upl[pl.ds(m, 1), :] = ext[0, pl.ds(floor_s[m], 1), :]
        return carry

    lax.fori_loop(0, BF // 8, gather_send, 0)
    fsend[...] = stage[...].astype(BF16)

    pl.semaphore_wait(barrier, N_DOM - 1 + N_SUB - 1 + 2)
    face_copies = []
    for side, there in ((0, before_id), (1, after_id)):
        copy = pltpu.make_async_remote_copy(
            src_ref=fsend.at[side],
            dst_ref=frecv.at[1 - side],
            send_sem=fsend_sem.at[side],
            recv_sem=frecv_sem.at[1 - side],
            device_id=there,
            device_id_type=MESH,
        )
        copy.start()
        face_copies.append(copy)

    lane = iota((1, 128), 1)
    moved = jnp.where(lane < NF, upl[...], 0.0)
    for shift in (16, 32, 64):
        moved = moved + pltpu.roll(moved, shift, 1)
    moved = moved.astype(BF16)
    places = iota((128, 1), 0) * 8
    packed = jnp.zeros((128, 128), F32)
    for p in range(8):
        hits = onehot(slots[...] == places + p)
        packed = packed + jnp.where(
            lax.shift_right_logical(lane, 4) == p, dot(hits, moved), 0.0
        )
    pack[...] = packed
    for d in range(N_DOM):
        asend[d] = pack[2 * d : 2 * d + 2, :]
    arecv[dom] = asend[dom]

    def send_floor(k, carry):
        there = lax.rem(dom + k, N_DOM)
        pltpu.make_async_remote_copy(
            src_ref=asend.at[there],
            dst_ref=arecv.at[dom],
            send_sem=asend_sem,
            recv_sem=arecv_sem,
            device_id=(there, sub),
            device_id_type=MESH,
        ).start()
        return carry

    lax.fori_loop(1, N_DOM, send_floor, 0)

    orow = iota((48, 1), 0)
    orow_v = div15(orow)
    orow_b = orow - NF * orow_v
    opick_v = onehot(orow_v == iota((48, NO), 1), F32)
    opick_b = onehot(orow_b == iota((48, NF), 1), F32)
    o_u = div5(lane)
    o_k = lane - NE * o_u
    o_ok = o_u < NO
    osel_k = onehot((o_k == iota((NE, 128), 0)) & o_ok, F32)
    osel_u = onehot((o_u == iota((NO, 128), 0)) & o_ok, F32)
    for v in range(NO):
        ost[NF * v : NF * (v + 1), :] = ocean[v]
    ost[NO * NF :, :] = jnp.zeros((48 - NO * NF, OC), F32)
    for g in range(3):
        proj = dot(opick_b, dot_tn(eproj[g], osel_k, HIGHEST), HIGHEST)
        proj = jnp.where((orow_v == o_u) & o_ok, proj, 0.0)
        oext[g * OC : (g + 1) * OC, :] = dot_tn(ost[...], proj, HIGHEST)
    for side in range(2):
        for j in range(OBF):
            osend[side, j : j + 1, :] = oext[pl.ds(osend_s[side, j], 1), :]
    ocean_copies = []
    for side, there in ((0, (dom_before, sub)), (1, (dom_after, sub))):
        copy = pltpu.make_async_remote_copy(
            src_ref=osend.at[side],
            dst_ref=orecv.at[1 - side],
            send_sem=osend_sem.at[side],
            recv_sem=orecv_sem.at[1 - side],
            device_id=there,
            device_id_type=MESH,
        )
        copy.start()
        ocean_copies.append(copy)

    stars = [star[d] for d in range(3)]
    eye = onehot(iota((NV, NV), 0) == iota((NV, NV), 1), F32)
    sel_u = onehot((q_u == iota((NV, 256), 0)) & q_ok)
    own = [None, None, None]
    for f in range(4):
        normal = 0.5 * (eye - combine(stars, TET[f]))
        lifts = dot(pick_b, dot(flift[f], sel_j).astype(BF16))
        mmat[:, f * 256 : (f + 1) * 256] = (spread(pick_v, normal, sel_u) * lifts).astype(
            BF16
        )
        through = dot(flift[f], fproj[f])
        for d, factor in TET[f]:
            term = through * -factor
            own[d] = term if own[d] is None else own[d] + term
    last = iota((1, ROWS), 1)
    last_u = div35(last)
    last_c = last - NB * last_u
    sel_u4 = onehot(last_u == iota((NV, ROWS), 0))
    sel_c4 = onehot(last_c == iota((NB, ROWS), 0))
    total = jnp.zeros((ROWS, ROWS), F32)
    for d in range(3):
        total = total + spread(pick_v, stars[d], sel_u4) * spread(pick_b, own[d], sel_c4)
    wmat[:, 3 * ROWS :] = total.astype(BF16)
    for c in range(E // CHUNK):
        cols = slice(c * CHUNK, (c + 1) * CHUNK)
        accf[:, cols] = xf[:, cols] + dot(wmat[...], xs[:, cols])

    for side in range(2):
        face_copies[side].wait_recv()
    has_before = (block > 0).astype(F32)
    has_after = (block < n_blocks - 1).astype(F32)
    ext[:, 4 * E : 4 * E + BF, :] = frecv[0].astype(F32) * has_before
    ext[:, 4 * E + BF : 4 * E + 2 * BF, :] = frecv[1].astype(F32) * has_after

    def gather(i, carry):
        for k in range(4):
            e = i * 4 + k
            for f in range(4):
                slot = nbr_s[f, e]
                for half in range(2):
                    beside[half, pl.ds(f * E + e, 1), :] = ext[half, pl.ds(slot, 1), :]
        return carry

    lax.fori_loop(0, E // 4, gather, 0)

    pltpu.make_async_copy(
        arecv.at[pl.ds(0, N_DOM - 1)], arecv.at[pl.ds(0, N_DOM - 1)], arecv_sem
    ).wait()
    for s in range(N_DOM):
        pack[2 * s : 2 * s + 2, :] = arecv[s]
    arrived = pack[...].astype(BF16)
    wide = iota((1, 1024), 1)
    wide_l = wide & 127
    wide_q = lax.shift_right_logical(wide, 7)
    pick_a = onehot(iota((128, 1), 0) == 8 * (wide_l & 15) + wide_q)
    targets = dot(arrival[...].astype(F32).astype(BF16), pick_a)
    targets = jnp.where(
        iota((8, 1), 0) == lax.shift_right_logical(wide_l, 4), targets, 0.0
    )
    targets = jnp.sum(targets, axis=0, keepdims=True)
    cells = iota((OC, 1), 0).astype(F32)
    forced = jnp.zeros((OC, 128), F32)
    for p in range(8):
        hits = onehot(targets[:, p * 128 : (p + 1) * 128] == cells)
        forced = forced + jnp.where(
            lax.shift_right_logical(lane, 4) == p, dot(hits, arrived), 0.0
        )
    fold = onehot((lane & 15) == iota((16, 128), 0), F32)
    part[sub] = dot_nt(fold, forced, HIGHEST)
    part_copies = []
    for k in range(1, N_SUB):
        copy = pltpu.make_async_remote_copy(
            src_ref=part.at[sub],
            dst_ref=part.at[sub],
            send_sem=psend_sem.at[k - 1],
            recv_sem=precv_sem.at[k - 1],
            device_id=(dom, lax.rem(sub + k, N_SUB)),
            device_id_type=MESH,
        )
        copy.start()
        part_copies.append(copy)

    rates = jnp.transpose(jnp.broadcast_to(strength[...], (128, 128)))
    rate_high, rate_low = split(rates)
    for f in range(4):
        on_fault = onehot(fault[...] == iota((E, 1), 0) + f * E)
        limit = dot(on_fault, rate_high) + dot(on_fault, rate_low)
        frictional = limit > 0.0
        inverse = 1.0 / jnp.where(frictional, limit, 1.0)
        for half in range(2):
            rows = slice(f * E, (f + 1) * E)
            jump = beside[half, rows, :] - ext[half, rows, :]
            jump = jnp.where(frictional, limit * jnp.tanh(jump * inverse), jump)
            jm[:, f * 256 + half * 128 : f * 256 + (half + 1) * 128] = jump.astype(BF16)
    for c in range(E // CHUNK):
        cols = slice(c * CHUNK, (c + 1) * CHUNK)
        accf[:, cols] = accf[:, cols] + dot_nt(mmat[...], jm[cols, :])
    for v in range(NV):
        out_e[v] = accf[NB * v : NB * (v + 1), :].astype(BF16)

    for side in range(2):
        ocean_copies[side].wait_recv()
    oext[3 * OC : 3 * OC + OBF, :] = orecv[0] * (dom > 0).astype(F32)
    oext[3 * OC + OBF :, :] = orecv[1] * (dom < N_DOM - 1).astype(F32)

    def ocean_gather(i, carry):
        for k in range(4):
            for g in range(3):
                obeside[pl.ds(g * OC + i * 4 + k, 1), :] = oext[
                    pl.ds(onbr_s[g, i * 4 + k], 1), :
                ]
        return carry

    lax.fori_loop(0, OC // 4, ocean_gather, 0)
    shals = [shal[d] for d in range(2)]
    oeye = onehot(iota((NO, NO), 0) == iota((NO, NO), 1), F32)
    inner = [okern[0], okern[1]]
    updated = ost[...]
    for g in range(3):
        through = dot(elift[g], eproj[g], HIGHEST)
        for d, factor in TRI[g]:
            inner[d] = inner[d] - factor * through
        normal = 0.25 * (oeye - combine(shals, TRI[g]))
        outer = dot(opick_v, dot(normal, osel_u, HIGHEST), HIGHEST)
        lifts = dot(opick_b, dot(elift[g], osel_k, HIGHEST), HIGHEST)
        ojump = obeside[g * OC : (g + 1) * OC, :] - oext[g * OC : (g + 1) * OC, :]
        updated = updated + dot_nt(outer * lifts, ojump, HIGHEST)
    volume = jnp.zeros((48, 48), F32)
    for d in range(2):
        left = dot_nt(dot(opick_v, shals[d], HIGHEST), opick_v, HIGHEST)
        right = dot_nt(dot(opick_b, inner[d], HIGHEST), opick_b, HIGHEST)
        volume = volume + left * right
    updated = updated + 0.5 * dot(volume, ost[...], HIGHEST)
    oacc[...] = updated
    for copy in part_copies:
        copy.wait_recv()
    source = part[0] + part[1] + part[2] + part[3]
    oacc[:16, :] = oacc[:16, :] + source
    for v in range(NO):
        out_o[v] = oacc[NF * v : NF * (v + 1), :]

    for copy in face_copies + ocean_copies + part_copies:
        copy.wait_send()
    pltpu.make_async_copy(
        asend.at[pl.ds(0, N_DOM - 1)], asend.at[pl.ds(0, N_DOM - 1)], asend_sem
    ).wait()


def body(
    elastic,
    jacobian,
    star_mats,
    stiffness,
    face_proj,
    face_lift,
    clusters,
    neighbours,
    send_faces,
    fault_faces,
    fault_strength,
    seafloor_faces,
    seafloor_slots,
    arrival_cells,
    ocean_state,
    ocean_kernels,
    shallow_mats,
    edge_proj,
    edge_lift,
    ocean_send,
    ocean_neighbours,
):
    vmem = pl.BlockSpec(memory_space=pltpu.VMEM)
    smem = pl.BlockSpec(memory_space=pltpu.SMEM)
    specs = [vmem] * 7 + [smem] * 2 + [vmem] * 2 + [smem] + [vmem] * 7 + [smem] * 2
    dma = pltpu.SemaphoreType.DMA
    return pl.pallas_call(
        kernel,
        out_shape=(
            jax.ShapeDtypeStruct(elastic.shape, BF16),
            jax.ShapeDtypeStruct(ocean_state.shape, F32),
        ),
        in_specs=specs,
        out_specs=(vmem, vmem),
        scratch_shapes=[
            pltpu.VMEM((ROWS, E), F32),
            pltpu.VMEM((4 * ROWS, E), BF16),
            pltpu.VMEM((ROWS, 4 * ROWS), BF16),
            pltpu.VMEM((ROWS, 1024), BF16),
            pltpu.VMEM((ROWS, 1024), BF16),
            pltpu.VMEM((2, 4 * E + 2 * BF, 128), F32),
            pltpu.VMEM((2, 4 * E, 128), F32),
            pltpu.VMEM((E, 1024), BF16),
            pltpu.VMEM((ROWS, E), F32),
            pltpu.VMEM((2, 2, BF, 128), F32),
            pltpu.VMEM((2, 2, BF, 128), BF16),
            pltpu.VMEM((2, 2, BF, 128), BF16),
            pltpu.VMEM((3 * OC + 2 * OBF, 128), F32),
            pltpu.VMEM((3 * OC, 128), F32),
            pltpu.VMEM((2, OBF, 128), F32),
            pltpu.VMEM((2, OBF, 128), F32),
            pltpu.VMEM((48, OC), F32),
            pltpu.VMEM((48, OC), F32),
            pltpu.VMEM((512, 128), F32),
            pltpu.VMEM((128, 128), F32),
            pltpu.VMEM((N_DOM, 2, 128), F32),
            pltpu.VMEM((N_DOM, 2, 128), F32),
            pltpu.VMEM((N_SUB, 16, OC), F32),
            dma((2,)),
            dma((2,)),
            dma((2,)),
            dma((2,)),
            dma,
            dma,
            dma((3,)),
            dma((3,)),
        ],
        compiler_params=pltpu.CompilerParams(
            collective_id=0,
            has_side_effects=True,
            vmem_limit_bytes=48 * 1024 * 1024,
        ),
    )(
        elastic,
        jacobian,
        star_mats,
        stiffness,
        face_proj,
        face_lift,
        clusters.reshape(1, E),
        neighbours,
        send_faces,
        fault_faces.reshape(1, 128),
        fault_strength.reshape(1, 128),
        seafloor_faces,
        seafloor_slots.reshape(1, 512),
        arrival_cells.reshape(8, 128),
        ocean_state,
        ocean_kernels,
        shallow_mats,
        edge_proj,
        edge_lift,
        ocean_send,
        ocean_neighbours,
    )


def solution(mesh):
    both = ("dom", "sub")
    return jax.shard_map(
        body,
        mesh=mesh,
        in_specs=(
            P(None, None, both),
            P(None, both),
            P(),
            P(),
            P(),
            P(),
            P(both),
            P(None, both),
            P(None, both),
            P(both),
            P(both),
            P(both),
            P(both),
            P(both),
            P(None, None, "dom"),
            P(),
            P(),
            P(),
            P(),
            P(None, "dom"),
            P(None, "dom"),
        ),
        out_specs=(P(None, None, both), P(None, None, "dom")),
        check_vma=False,
    )
```

profile of v0, /device:TPU:0, one launch (start us, length us, event | category | flops | bytes accessed | tf_op | source)
XLA Modules:
  0.0 40.0 jit_solution(680670874181716440)
XLA Ops:
  0.7 0.7 %copy.27.shal = f32[2,3,3]{2,1,0:T(4,128)S(1)} copy(f32[2,3,3]{2,0,1:T(2,128)} %param.37) | data formatting | bytes 144 | tf_op args[16]
  1.4 0.0 copy-done.15
  1.4 0.0 copy-start.17
  1.4 0.7 %copy-done.16 = f32[2,15,15]{2,0,1:T(2,128)S(1)} copy-done((f32[2,15,15]{2,0,1:T(2,128)S(1)}, f32[2,15,15]{2,0,1:T(2,128)}, u32[]{:S(2)}) %copy-start.16) | copy-done | bytes 1824
  2.1 0.7 %copy-done.14 = f32[3,9,9]{2,0,1:T(4,128)S(1)} copy-done((f32[3,9,9]{2,0,1:T(4,128)S(1)}, f32[3,9,9]{2,0,1:T(4,128)}, u32[]{:S(2)}) %copy-start.14) | copy-done | bytes 996
  2.8 0.0 copy-start.10
  2.8 0.0 copy-start.12
  2.8 0.0 copy-start.13
  2.9 0.0 copy-start.1
  2.9 0.1 copy.29.elift
  3.0 0.0 copy-start.6
  3.0 0.0 copy-start.8
  3.0 0.0 copy-start.11
  3.0 0.1 copy.25.flift
  3.2 0.3 copy-done.3
  3.5 0.0 copy-done.4
  3.5 0.0 copy-done.10
  3.6 0.2 copy-done.1
  3.7 0.0 copy-done.2
  3.8 0.0 copy-start
  3.8 1.1 %copy-done = bf16[9,35,1024]{2,1,0:T(8,128)(2,1)S(1)} copy-done((bf16[9,35,1024]{2,1,0:T(8,128)(2,1)S(1)}, bf16[9,35,1024]{2,1,0:T(8,128)(2,1)}, u32[]{:S(2)}) %copy-start) | copy-done | bytes 645144
  4.9 33.6 %shard_map.212 = (bf16[9,35,1024]{2,1,0:T(8,128)(2,1)S(1)}, f32[3,15,256]{2,1,0:T(8,128)S(1)}) custom-call(bf16[9,35,1024]{2,1,0:T(8,128)(2,1)S(1)} %copy-done, f32[3,1024]{1,0:T(4,128)S(1)} %copy-done.3, f32[3,9,9]{2,1,0:T(8,128)S(1)} %copy.23.star, bf16[3,35,35]{2,1,0:T(8,128)(2,1)S(1)} %copy-done.2, bf16[4,15,35]{2,1,0:T(8,128)(2,1)S(1)} %copy.24.fproj, ...), custom_call_target="tpu_custom_call" | custom-call | tf_op jit(solution)/shard_map/pallas_call | solution.py:514
  38.5 0.9 %copy.32 = bf16[9,35,1024]{2,1,0:T(8,128)(2,1)} copy(bf16[9,35,1024]{2,1,0:T(8,128)(2,1)S(1)} %get-tuple-element.4) | data formatting | bytes 1290240
  39.4 0.6 %copy.33 = f32[3,15,256]{2,1,0:T(8,128)} copy(f32[3,15,256]{2,1,0:T(8,128)S(1)} %get-tuple-element.5) | data formatting | bytes 92160
  (26 shorter events, 0.1 us)
Async XLA Ops:
  0.6 0.7 %copy-start.18 = (f32[3,5,15]{2,0,1:T(4,128)S(1)}, f32[3,5,15]{2,0,1:T(4,128)}, u32[]{:S(2)}) copy-start(f32[3,5,15]{2,0,1:T(4,128)} %param.38) | copy-start | bytes 2704
  0.6 0.7 %copy-start.15 = (bf16[4,15,35]{2,0,1:T(4,128)(2,1)S(1)}, bf16[4,15,35]{2,0,1:T(4,128)(2,1)}, u32[]{:S(2)}) copy-start(bf16[4,15,35]{2,0,1:T(4,128)(2,1)} %param.25) | copy-start | bytes 12604
  1.4 0.7 %copy-start.16 = (f32[2,15,15]{2,0,1:T(2,128)S(1)}, f32[2,15,15]{2,0,1:T(2,128)}, u32[]{:S(2)}) copy-start(f32[2,15,15]{2,0,1:T(2,128)} %param.36) | copy-start | bytes 5404
  1.4 1.6 %copy-start.17 = (bf16[4,35,15]{1,0,2:T(4,128)(2,1)S(1)}, bf16[4,35,15]{1,0,2:T(4,128)(2,1)}, u32[]{:S(2)}) copy-start(bf16[4,35,15]{1,0,2:T(4,128)(2,1)} %param.26) | copy-start | bytes 12604
  2.1 0.7 %copy-start.14 = (f32[3,9,9]{2,0,1:T(4,128)S(1)}, f32[3,9,9]{2,0,1:T(4,128)}, u32[]{:S(2)}) copy-start(f32[3,9,9]{2,0,1:T(4,128)} %param.23) | copy-start | bytes 2920
  2.1 0.8 %copy-start.19 = (f32[3,15,5]{1,0,2:T(4,128)S(1)}, f32[3,15,5]{1,0,2:T(4,128)}, u32[]{:S(2)}) copy-start(f32[3,15,5]{1,0,2:T(4,128)} %param.39) | copy-start | bytes 2704
  2.8 0.7 %copy-start.3 = (f32[3,1024]{1,0:T(4,128)S(1)}, f32[3,1024]{1,0:T(4,128)}, u32[]{:S(2)}) copy-start(f32[3,1024]{1,0:T(4,128)} %jac.1) | copy-start | bytes 36868
  2.8 0.7 %copy-start.4 = (s32[4,1024]{1,0:T(4,128)S(1)}, s32[4,1024]{1,0:T(4,128)}, u32[]{:S(2)}) copy-start(s32[4,1024]{1,0:T(4,128)} %nbr_s.1) | copy-start | bytes 49156
  2.8 0.7 %copy-start.7 = (s32[3,256]{1,0:T(4,128)S(1)}, s32[3,256]{1,0:T(4,128)}, u32[]{:S(2)}) copy-start(s32[3,256]{1,0:T(4,128)} %onbr_s.1) | copy-start | bytes 9220
  2.8 0.7 %copy-start.9 = (s32[512]{0:T(512)S(1)}, s32[512]{0:T(512)}, u32[]{:S(2)}) copy-start(s32[512]{0:T(512)} %floor_s.1) | copy-start | bytes 6148
  2.8 0.7 %copy-start.10 = (s32[512]{0:T(512)S(1)}, s32[512]{0:T(512)}, u32[]{:S(2)}) copy-start(s32[512]{0:T(512)} %param.33) | copy-start | bytes 6148
  2.8 0.7 %copy-start.12 = (s32[128]{0:T(128)S(1)}, s32[128]{0:T(128)}, u32[]{:S(2)}) copy-start(s32[128]{0:T(128)} %param.30) | copy-start | bytes 1540
  2.8 0.7 %copy-start.13 = (f32[128]{0:T(128)S(1)}, f32[128]{0:T(128)}, u32[]{:S(2)}) copy-start(f32[128]{0:T(128)} %param.31) | copy-start | bytes 1540
  2.9 0.8 %copy-start.1 = (f32[3,15,256]{2,1,0:T(8,128)S(1)}, f32[3,15,256]{2,1,0:T(8,128)}, u32[]{:S(2)}) copy-start(f32[3,15,256]{2,1,0:T(8,128)} %ocean.1) | copy-start | bytes 138244
  3.0 0.8 %copy-start.2 = (bf16[3,35,35]{2,1,0:T(8,128)(2,1)S(1)}, bf16[3,35,35]{2,1,0:T(8,128)(2,1)}, u32[]{:S(2)}) copy-start(bf16[3,35,35]{2,1,0:T(8,128)(2,1)} %stiff.1) | copy-start | bytes 22054
  3.0 0.8 %copy-start.5 = (s32[1024]{0:T(1024)S(1)}, s32[1024]{0:T(1024)}, u32[]{:S(2)}) copy-start(s32[1024]{0:T(1024)} %param.27) | copy-start | bytes 12292
  3.0 0.8 %copy-start.6 = (s32[1024]{0:T(1024)S(1)}, s32[1024]{0:T(1024)}, u32[]{:S(2)}) copy-start(s32[1024]{0:T(1024)} %param.34) | copy-start | bytes 12292
  3.0 0.7 %copy-start.8 = (s32[2,256]{1,0:T(2,128)S(1)}, s32[2,256]{1,0:T(2,128)}, u32[]{:S(2)}) copy-start(s32[2,256]{1,0:T(2,128)} %send_s.1) | copy-start | bytes 6148
  3.0 0.7 %copy-start.11 = (s32[2,32]{1,0:T(2,128)S(1)}, s32[2,32]{1,0:T(2,128)}, u32[]{:S(2)}) copy-start(s32[2,32]{1,0:T(2,128)} %osend_s.1) | copy-start | bytes 772
  3.8 1.1 %copy-start = (bf16[9,35,1024]{2,1,0:T(8,128)(2,1)S(1)}, bf16[9,35,1024]{2,1,0:T(8,128)(2,1)}, u32[]{:S(2)}) copy-start(bf16[9,35,1024]{2,1,0:T(8,128)(2,1)} %elastic.1) | copy-start | bytes 1935364
where the time goes:
time: 40.3 us; the launch traced here: 40 us
  Pallas kernels  33.6 us (83%)
  local copies, waits for them, and re-layouts  5.59 us (14%)
  between operations  0.79 us (2%)
    pallas_call x1, Pallas kernels, body(): pl.pallas_call(kernel, out_shape=(jax.ShapeDtypeStruct(elastic.shape, BF1...  33.6 us
    unnamed x49, local copies, waits for them, and re-layouts  5.59 us

commit v1 on v0

v1 whole, which is shorter than its diff:
```python
import functools

import jax
import jax.numpy as jnp
from jax import lax
from jax.experimental import pallas as pl
from jax.experimental.pallas import tpu as pltpu
from jax.sharding import PartitionSpec as P

MESH = pl.DeviceIdType.MESH
F32, BF16 = jnp.float32, jnp.bfloat16
HIGHEST = lax.Precision.HIGHEST

NV, NB, NF = 9, 35, 15
NO, NE = 3, 5
ROWS = 320
E = 1024
BF = 256
OC, OBF = 256, 32
CAP = 16
N_DOM, N_SUB = 64, 4
CHUNK = 256
MAIN = 128
LEAD = 8
REST = 4 * E + 2 * BF + 2 * LEAD
ROOT3 = 0.57735027
ROOT2 = 0.70710678
TET = [
    [(2, -1.0)],
    [(1, -1.0)],
    [(0, -1.0)],
    [(0, ROOT3), (1, ROOT3), (2, ROOT3)],
]
TRI = [[(1, -1.0)], [(0, -1.0)], [(0, ROOT2), (1, ROOT2)]]


def iota(shape, dim):
    return lax.broadcasted_iota(jnp.int32, shape, dim)


def div35(x):
    return lax.shift_right_logical(x * 1873, 16)


def div15(x):
    return lax.shift_right_logical(x * 4370, 16)


def div5(x):
    return lax.shift_right_logical(x * 13108, 16)


def onehot(cond, dtype=BF16):
    return jnp.where(cond, 1.0, 0.0).astype(dtype)


def dot(a, b, precision=None):
    return lax.dot_general(
        a, b, (((1,), (0,)), ((), ())), precision=precision, preferred_element_type=F32
    )


def dot_tn(a, b, precision=None):
    return lax.dot_general(
        a, b, (((0,), (0,)), ((), ())), precision=precision, preferred_element_type=F32
    )


def dot_nt(a, b, precision=None):
    return lax.dot_general(
        a, b, (((1,), (1,)), ((), ())), precision=precision, preferred_element_type=F32
    )


def split(x):
    high = x.astype(BF16)
    return high, (x - high.astype(F32)).astype(BF16)


def combine(mats, pairs):
    total = None
    for direction, factor in pairs:
        term = mats[direction] * factor
        total = term if total is None else total + term
    return total


def spread(select_rows, mat, select_cols):
    return dot(select_rows, dot(mat.astype(BF16), select_cols).astype(BF16))


def face_columns(q):
    group = div15(q)
    variable = jnp.where(group == 0, NV - 1, group - 1)
    return variable, q - NF * group, group < NV


def main_kernel(
    elastic_h,
    jac_h,
    star_h,
    stiff_h,
    fproj_h,
    flift_h,
    clusters_h,
    nbr_h,
    send_h,
    fault_h,
    strength_h,
    floor_h,
    slots_h,
    arrival_h,
    ocean_h,
    okern_h,
    shal_h,
    eproj_h,
    elift_h,
    osend_h,
    onbr_h,
    fault1_h,
    out_e_h,
    out_o_h,
    elastic,
    jac,
    star,
    stiff,
    fproj,
    flift,
    clusters,
    nbr_s,
    send_s,
    fault,
    fault_s,
    strength,
    floor_s,
    slots,
    arrival,
    ocean,
    okern,
    shal,
    eproj,
    elift,
    osend_s,
    onbr_s,
    in_sem,
    xf,
    xs,
    wmat,
    fmat,
    mmat,
    accf,
    ext,
    jm,
    fjump,
    fjump_rest,
    fsend,
    frecv,
    out_e,
    out_o,
    oacc,
    oext,
    obeside,
    osend,
    orecv,
    ost,
    upl,
    pack,
    asend,
    arecv,
    part,
    fsend_sem,
    frecv_sem,
    osend_sem,
    orecv_sem,
    asend_sem,
    arecv_sem,
    psend_sem,
    precv_sem,
    out_sem,
):
    loads = {}
    pairs = (
        ("star", star_h, star),
        ("stiff", stiff_h, stiff),
        ("elastic", elastic_h, elastic),
        ("jac", jac_h, jac),
        ("clusters", clusters_h, clusters),
        ("fproj", fproj_h, fproj),
        ("floor", floor_h, floor_s),
        ("slots", slots_h, slots),
        ("send_s", send_h, send_s),
        ("nbr_s", nbr_h, nbr_s),
        ("flift", flift_h, flift),
        ("arrival", arrival_h, arrival),
        ("fault", fault_h, fault),
        ("fault_s", fault1_h, fault_s),
        ("strength", strength_h, strength),
        ("ocean", ocean_h, ocean),
        ("eproj", eproj_h, eproj),
        ("osend", osend_h, osend_s),
        ("onbr", onbr_h, onbr_s),
        ("okern", okern_h, okern),
        ("shal", shal_h, shal),
        ("elift", elift_h, elift),
    )
    for n, (name, source, target) in enumerate(pairs):
        loads[name] = pltpu.make_async_copy(source, target, in_sem.at[n])
        loads[name].start()

    dom = lax.axis_index("dom")
    sub = lax.axis_index("sub")
    block = dom * N_SUB + sub
    n_blocks = N_DOM * N_SUB
    after = lax.rem(block + 1, n_blocks)
    before = lax.rem(block + n_blocks - 1, n_blocks)
    after_id = (lax.div(after, N_SUB), lax.rem(after, N_SUB))
    before_id = (lax.div(before, N_SUB), lax.rem(before, N_SUB))
    dom_after = lax.rem(dom + 1, N_DOM)
    dom_before = lax.rem(dom + N_DOM - 1, N_DOM)

    barrier = pltpu.get_barrier_semaphore()

    def greet(i, carry):
        for k in range(1, 10):
            there = (lax.rem(dom + i * 9 + k, N_DOM), sub)
            pl.semaphore_signal(barrier, inc=1, device_id=there, device_id_type=MESH)
        return carry

    lax.fori_loop(0, 7, greet, 0)
    for k in range(1, N_SUB):
        there = (dom, lax.rem(sub + k, N_SUB))
        pl.semaphore_signal(barrier, inc=1, device_id=there, device_id_type=MESH)
    for there in (before_id, after_id):
        pl.semaphore_signal(barrier, inc=1, device_id=there, device_id_type=MESH)

    row = iota((ROWS, 1), 0)
    row_v = div35(row)
    row_b = row - NB * row_v
    pick_v = onehot(row_v == iota((ROWS, NV), 1))
    pick_b = onehot(row_b == iota((ROWS, NB), 1))

    col = iota((1, 3 * ROWS), 1)
    col_d = (col >= ROWS).astype(jnp.int32) + (col >= 2 * ROWS).astype(jnp.int32)
    col_r = col - ROWS * col_d
    col_u = div35(col_r)
    col_c = col_r - NB * col_u
    loads["star"].wait()
    loads["stiff"].wait()
    stars = [star[:, d, :] for d in range(3)]
    a_cols, k_cols = None, None
    for d in range(3):
        sel_u = onehot((col_d == d) & (col_u == iota((NV, 3 * ROWS), 0)))
        sel_c = onehot((col_d == d) & (col_c == iota((NB, 3 * ROWS), 0)))
        terms = (dot(stars[d].astype(BF16), sel_u), dot(stiff[d], sel_c))
        if d == 0:
            a_cols, k_cols = terms
        else:
            a_cols, k_cols = a_cols + terms[0], k_cols + terms[1]
    wmat[:, : 3 * ROWS] = (
        dot(pick_v, a_cols.astype(BF16)) * dot(pick_b, k_cols.astype(BF16))
    ).astype(BF16)

    loads["elastic"].wait()
    for v in range(NV):
        xf[NB * v : NB * (v + 1), :] = elastic[v].astype(F32)
    xf[NV * NB :, :] = jnp.zeros((ROWS - NV * NB, E), F32)
    loads["jac"].wait()
    loads["clusters"].wait()
    step = 0.5 * jnp.exp2(-clusters[...].astype(F32))
    chunks = [slice(c * CHUNK, (c + 1) * CHUNK) for c in range(E // CHUNK)]

    def scaled(x, cols):
        for d in range(3):
            xs[d * ROWS : (d + 1) * ROWS, cols] = (jac[d : d + 1, cols] * x).astype(BF16)

    for cols in chunks:
        scaled(xf[:, cols], cols)

    loads["fproj"].wait()
    fprojs = fproj[...].astype(F32)
    fprojs = [fprojs[:, f, :].astype(BF16) for f in range(4)]
    lane = iota((1, 128), 1)
    q_u, q_j, q_ok = face_columns(lane)
    r_lane = lane & 31
    r_u, r_j, r_ok = face_columns(MAIN + r_lane)
    r_ok = r_ok & (r_lane < 8)
    halves = ((q_u, q_j, q_ok), (r_u, r_j, r_ok))
    sel_j = [onehot((h_j == iota((NF, MAIN), 0)) & h_ok) for h_u, h_j, h_ok in halves]
    for half, (h_u, h_j, h_ok) in enumerate(halves):
        pair_u = jnp.concatenate([jnp.where(h_ok, h_u, -1)] * 2, axis=1)
        for f in range(0, 4, 2):
            proj = [dot_tn(fprojs[f + n], sel_j[half]).astype(BF16) for n in range(2)]
            proj = dot(pick_b, jnp.concatenate(proj, axis=1))
            fmat[:, (4 * half + f) * MAIN : (4 * half + f + 2) * MAIN] = jnp.where(
                row_v == pair_u, proj, 0.0
            ).astype(BF16)

    for cols in chunks:
        h = step[:, cols]
        term = dot(wmat[:, : 3 * ROWS], xs[: 3 * ROWS, cols])
        accf[:, cols] = h * xf[:, cols] + (h * h * 0.5) * term
        scaled(term, cols)
    for cols in chunks:
        h = step[:, cols]
        term = dot(wmat[:, : 3 * ROWS], xs[: 3 * ROWS, cols])
        integral = (accf[:, cols] + (h * h * h * (1.0 / 6.0)) * term).astype(BF16)
        xs[3 * ROWS :, cols] = integral
    for c, cols in enumerate(chunks):
        traced = dot_tn(xs[3 * ROWS :, cols], fmat[...])
        for f in range(4):
            rows = slice(LEAD + f * E + c * CHUNK, LEAD + f * E + (c + 1) * CHUNK)
            ext[rows, :] = traced[:, f * MAIN : (f + 1) * MAIN]
            rows = slice(REST + rows.start, REST + rows.stop)
            ext[rows, :] = traced[:, (4 + f) * MAIN : (5 + f) * MAIN]

    sublane = iota((8, 128), 0)

    def rows8(table, slots8, start=LEAD):
        taken = table[pl.ds(slots8[0] + start, 8), :]
        for k in range(1, 8):
            taken = jnp.where(
                sublane == k, table[pl.ds(slots8[k] + (start - k), 8), :], taken
            )
        return taken

    loads["floor"].wait()
    loads["slots"].wait()
    loads["send_s"].wait()

    def gather_floor(i, carry):
        for k in range(4):
            first = pl.multiple_of(i * 32 + 8 * k, 8)
            upl[pl.ds(first, 8), :] = rows8(ext, [floor_s[first + n] for n in range(8)])
        return carry

    lax.fori_loop(0, 512 // 32, gather_floor, 0)
    moved = jnp.where(lane < NF, upl[...], 0.0)
    for shift in (16, 32, 64):
        moved = moved + pltpu.roll(moved, shift, 1)
    moved = moved.astype(BF16)
    places = iota((128, 1), 0) * 8
    packed = jnp.zeros((128, 128), F32)
    for p in range(8):
        hits = onehot(slots[...] == places + p)
        packed = packed + jnp.where(
            lax.shift_right_logical(lane, 4) == p, dot(hits, moved), 0.0
        )
    pack[...] = packed
    for d in range(N_DOM):
        asend[d] = pack[2 * d : 2 * d + 2, :]
    arecv[dom] = asend[dom]

    pl.semaphore_wait(barrier, N_DOM - 1 + N_SUB - 1 + 2)

    def send_floor(i, carry):
        for k in range(1, 10):
            there = lax.rem(dom + i * 9 + k, N_DOM)
            pltpu.make_async_remote_copy(
                src_ref=asend.at[there],
                dst_ref=arecv.at[dom],
                send_sem=asend_sem,
                recv_sem=arecv_sem,
                device_id=(there, sub),
                device_id_type=MESH,
            ).start()
        return carry

    lax.fori_loop(0, 7, send_floor, 0)

    for part_ in range(BF // 128):

        def gather_send(i, carry):
            first = pl.multiple_of(i * 16, 16)
            for side in range(2):
                slots = [send_s[part_ * 256 + side * 128 + first + n] for n in range(16)]
                for half, start in enumerate((LEAD, LEAD + REST)):
                    taken = [rows8(ext, slots[8 * h : 8 * h + 8], start) for h in range(2)]
                    rows = pl.ds(part_ * 128 + first, 16)
                    fsend[side, half, rows, :] = jnp.concatenate(taken, axis=0).astype(BF16)
            return carry

        lax.fori_loop(0, 128 // 16, gather_send, 0)
    face_copies = []
    for side, there in ((0, before_id), (1, after_id)):
        copy = pltpu.make_async_remote_copy(
            src_ref=fsend.at[side],
            dst_ref=frecv.at[1 - side],
            send_sem=fsend_sem.at[side],
            recv_sem=frecv_sem.at[1 - side],
            device_id=there,
            device_id_type=MESH,
        )
        copy.start()
        face_copies.append(copy)

    orow = iota((48, 1), 0)
    orow_v = div15(orow)
    orow_b = orow - NF * orow_v
    opick_v = onehot(orow_v == iota((48, NO), 1), F32)
    opick_b = onehot(orow_b == iota((48, NF), 1), F32)
    o_u = div5(lane)
    o_k = lane - NE * o_u
    o_ok = o_u < NO
    osel_k = onehot((o_k == iota((NE, 128), 0)) & o_ok, F32)
    osel_u = onehot((o_u == iota((NO, 128), 0)) & o_ok, F32)
    loads["ocean"].wait()
    loads["eproj"].wait()
    loads["osend"].wait()
    for v in range(NO):
        ost[NF * v : NF * (v + 1), :] = ocean[v]
    ost[NO * NF :, :] = jnp.zeros((48 - NO * NF, OC), F32)
    eprojs = [eproj[:, g, :] for g in range(3)]
    for g in range(3):
        proj = dot(opick_b, dot_tn(eprojs[g], osel_k, HIGHEST), HIGHEST)
        proj = jnp.where((orow_v == o_u) & o_ok, proj, 0.0)
        oext[LEAD + g * OC : LEAD + (g + 1) * OC, :] = dot_tn(ost[...], proj, HIGHEST)
    for side in range(2):
        for j in range(OBF):
            osend[side, j : j + 1, :] = oext[pl.ds(osend_s[side, j] + LEAD, 1), :]
    ocean_copies = []
    for side, there in ((0, (dom_before, sub)), (1, (dom_after, sub))):
        copy = pltpu.make_async_remote_copy(
            src_ref=osend.at[side],
            dst_ref=orecv.at[1 - side],
            send_sem=osend_sem.at[side],
            recv_sem=orecv_sem.at[1 - side],
            device_id=there,
            device_id_type=MESH,
        )
        copy.start()
        ocean_copies.append(copy)

    loads["flift"].wait()
    flifts = flift[...].astype(F32)
    flifts = [flifts[:, f, :].astype(BF16) for f in range(4)]
    eye = onehot(iota((NV, NV), 0) == iota((NV, NV), 1), F32)
    sel_u = [onehot((h_u == iota((NV, MAIN), 0)) & h_ok) for h_u, h_j, h_ok in halves]
    sel_u = jnp.concatenate(sel_u, axis=1)
    sel_jj = jnp.concatenate(sel_j, axis=1)
    own = [None, None, None]
    mrest = jnp.zeros((ROWS, MAIN), F32)
    for f in range(4):
        normal = 0.5 * (eye - combine(stars, TET[f]))
        both = spread(pick_v, normal, sel_u) * dot(
            pick_b, dot_tn(flifts[f], sel_jj).astype(BF16)
        )
        mmat[:, f * MAIN : (f + 1) * MAIN] = both[:, :MAIN].astype(BF16)
        mrest = mrest + jnp.where(
            lax.shift_right_logical(lane, 5) == f, both[:, MAIN:], 0.0
        )
        through = dot_tn(flifts[f], fprojs[f])
        for d, factor in TET[f]:
            term = through * -factor
            own[d] = term if own[d] is None else own[d] + term
    mmat[:, 4 * MAIN :] = mrest.astype(BF16)
    last = iota((1, ROWS), 1)
    last_u = div35(last)
    last_c = last - NB * last_u
    sel_u4 = onehot(last_u == iota((NV, ROWS), 0))
    sel_c4 = onehot(last_c == iota((NB, ROWS), 0))
    total = jnp.zeros((ROWS, ROWS), F32)
    for d in range(3):
        total = total + spread(pick_v, stars[d], sel_u4) * spread(pick_b, own[d], sel_c4)
    wmat[:, 3 * ROWS :] = total.astype(BF16)
    for cols in chunks:
        scaled(xs[3 * ROWS :, cols].astype(F32), cols)
    for cols in chunks:
        accf[:, cols] = xf[:, cols] + dot(wmat[...], xs[:, cols])

    loads["arrival"].wait()
    wide = iota((1, 1024), 1)
    wide_l = wide & 127
    wide_q = lax.shift_right_logical(wide, 7)
    pick_a = onehot(iota((128, 1), 0) == 8 * (wide_l & 15) + wide_q)
    targets = dot(arrival[...].astype(F32).astype(BF16), pick_a)
    targets = jnp.where(
        iota((8, 1), 0) == lax.shift_right_logical(wide_l, 4), targets, 0.0
    )
    targets = jnp.sum(targets, axis=0, keepdims=True)
    cells = iota((OC, 1), 0).astype(F32)
    pltpu.make_async_copy(
        arecv.at[pl.ds(0, N_DOM - 1)], arecv.at[pl.ds(0, N_DOM - 1)], arecv_sem
    ).wait()
    for s in range(N_DOM):
        pack[2 * s : 2 * s + 2, :] = arecv[s]
    arrived = pack[...].astype(BF16)
    forced = jnp.zeros((OC, 128), F32)
    for p in range(8):
        hits = onehot(targets[:, p * 128 : (p + 1) * 128] == cells)
        forced = forced + jnp.where(
            lax.shift_right_logical(lane, 4) == p, dot(hits, arrived), 0.0
        )
    fold = onehot((lane & 15) == iota((16, 128), 0), F32)
    part[sub] = dot_nt(fold, forced, HIGHEST)
    part_copies = []
    for k in range(1, N_SUB):
        copy = pltpu.make_async_remote_copy(
            src_ref=part.at[sub],
            dst_ref=part.at[sub],
            send_sem=psend_sem.at[k - 1],
            recv_sem=precv_sem.at[k - 1],
            device_id=(dom, lax.rem(sub + k, N_SUB)),
            device_id_type=MESH,
        )
        copy.start()
        part_copies.append(copy)

    for copy in face_copies:
        copy.wait_recv()
    has_before = (block > 0).astype(F32)
    has_after = (block < n_blocks - 1).astype(F32)
    for half in range(2):
        first = half * REST + LEAD + 4 * E
        ext[first : first + BF, :] = frecv[0, half].astype(F32) * has_before
        ext[first + BF : first + 2 * BF, :] = frecv[1, half].astype(F32) * has_after

    loads["nbr_s"].wait()
    face_lane = lax.shift_right_logical(iota((8, 128), 1), 5)

    def gather_block(block8, carry):
        def gather(i, carry):
            rests = []
            mains = [[], [], [], []]
            near_first = block8 * 512 + i * 16
            for h in range(2):
                e = pl.multiple_of(block8 * 128 + i * 16 + 8 * h, 8)
                rest = None
                for f in range(4):
                    slots8 = [nbr_s[near_first + (f * 128 + 8 * h + n)] for n in range(8)]
                    own_row = LEAD + f * E + e
                    mains[f].append(
                        rows8(ext, slots8) - ext[pl.ds(pl.multiple_of(own_row, 8), 8), :]
                    )
                    own_row = pl.multiple_of(own_row + REST, 8)
                    jump = rows8(ext, slots8, LEAD + REST) - ext[pl.ds(own_row, 8), :]
                    rest = jump if f == 0 else jnp.where(face_lane == f, jump, rest)
                rests.append(rest)
            rows = pl.ds(pl.multiple_of(block8 * 128 + i * 16, 16), 16)
            for f in range(4):
                jm[rows, f * MAIN : (f + 1) * MAIN] = jnp.concatenate(
                    mains[f], axis=0
                ).astype(BF16)
            jm[rows, 4 * MAIN :] = jnp.concatenate(rests, axis=0).astype(BF16)
            return carry

        return lax.fori_loop(0, 128 // 16, gather, carry)

    lax.fori_loop(0, E // 128, gather_block, 0)

    loads["fault"].wait()
    loads["fault_s"].wait()
    loads["strength"].wait()

    def gather_fault(i, carry):
        first = pl.multiple_of(i * 8, 8)
        near = [fault_s[first + n] for n in range(8)]
        far = [
            nbr_s[
                jnp.bitwise_and(lax.shift_right_logical(slot, 7), 7) * 512
                + lax.shift_right_logical(slot, 10) * 128
                + jnp.bitwise_and(slot, 127)
            ]
            for slot in near
        ]
        rows = pl.ds(first, 8)
        fjump[rows, :] = rows8(ext, far) - rows8(ext, near)
        fjump_rest[rows, :] = rows8(ext, far, LEAD + REST) - rows8(ext, near, LEAD + REST)
        return carry

    lax.fori_loop(0, 128 // 8, gather_fault, 0)
    limit = jnp.transpose(jnp.broadcast_to(strength[...], (128, 128)))
    faults = jnp.transpose(jnp.broadcast_to(fault[...].astype(F32), (128, 128)))
    faults = faults.astype(jnp.int32)
    fault_face = lax.shift_right_logical(faults, 10)
    inverse = 1.0 / limit
    change = limit * jnp.tanh(fjump[...] * inverse) - fjump[...]
    change_rest = limit * jnp.tanh(fjump_rest[...] * inverse) - fjump_rest[...]
    changes = [jnp.where(fault_face == f, change, 0.0) for f in range(4)]
    changes.append(
        jnp.where(fault_face == lax.shift_right_logical(lane, 5), change_rest, 0.0)
    )
    changes = jnp.concatenate(changes, axis=1).astype(BF16)
    lifted = dot_nt(mmat[...], changes).astype(BF16)
    fault_elem = (faults & (E - 1))[:, :1]

    out_copies = []
    for c, cols in enumerate(chunks):
        at = onehot(fault_elem == iota((1, CHUNK), 1) + c * CHUNK)
        accf[:, cols] = accf[:, cols] + dot_nt(mmat[...], jm[cols, :]) + dot(lifted, at)
        for v in range(NV):
            out_e[v, :, cols] = accf[NB * v : NB * (v + 1), cols].astype(BF16)
        copy = pltpu.make_async_copy(
            out_e.at[:, :, cols], out_e_h.at[:, :, cols], out_sem.at[c]
        )
        copy.start()
        out_copies.append(copy)

    loads["onbr"].wait()
    loads["okern"].wait()
    loads["shal"].wait()
    loads["elift"].wait()
    for side in range(2):
        ocean_copies[side].wait_recv()
    first = LEAD + 3 * OC
    oext[first : first + OBF, :] = orecv[0] * (dom > 0).astype(F32)
    oext[first + OBF : first + 2 * OBF, :] = orecv[1] * (dom < N_DOM - 1).astype(F32)

    for part_ in range(OC // 128):

        def ocean_gather(i, carry):
            for g in range(3):
                slots8 = [onbr_s[part_, g, i * 8 + n] for n in range(8)]
                rows = pl.ds(pl.multiple_of(g * OC + part_ * 128 + i * 8, 8), 8)
                obeside[rows, :] = rows8(oext, slots8)
            return carry

        lax.fori_loop(0, 128 // 8, ocean_gather, 0)
    shals = [shal[:, d, :] for d in range(2)]
    elifts = [elift[:, g, :] for g in range(3)]
    oeye = onehot(iota((NO, NO), 0) == iota((NO, NO), 1), F32)
    inner = [okern[:, d, :] for d in range(2)]
    updated = ost[...]
    for g in range(3):
        through = dot_tn(elifts[g], eprojs[g], HIGHEST)
        for d, factor in TRI[g]:
            inner[d] = inner[d] - factor * through
        normal = 0.25 * (oeye - combine(shals, TRI[g]))
        outer = dot(opick_v, dot(normal, osel_u, HIGHEST), HIGHEST)
        lifts = dot(opick_b, dot_tn(elifts[g], osel_k, HIGHEST), HIGHEST)
        ojump = obeside[g * OC : (g + 1) * OC, :] - oext[LEAD + g * OC : LEAD + (g + 1) * OC, :]
        updated = updated + dot_nt(outer * lifts, ojump, HIGHEST)
    volume = jnp.zeros((48, 48), F32)
    for d in range(2):
        left = dot_nt(dot(opick_v, shals[d], HIGHEST), opick_v, HIGHEST)
        right = dot_nt(dot(opick_b, inner[d], HIGHEST), opick_b, HIGHEST)
        volume = volume + left * right
    oacc[...] = updated + 0.5 * dot(volume, ost[...], HIGHEST)

    for copy in part_copies:
        copy.wait_recv()
    oacc[:16, :] = oacc[:16, :] + (part[0] + part[1] + part[2] + part[3])
    for v in range(NO):
        out_o[v] = oacc[NF * v : NF * (v + 1), :]
    copy = pltpu.make_async_copy(out_o, out_o_h, out_sem.at[E // CHUNK])
    copy.start()
    out_copies.append(copy)

    for copy in face_copies + ocean_copies + part_copies:
        copy.wait_send()
    pltpu.make_async_copy(
        asend.at[pl.ds(0, N_DOM - 1)], asend.at[pl.ds(0, N_DOM - 1)], asend_sem
    ).wait()
    for copy in out_copies:
        copy.wait()


def place_kernel(elastic, ocean, out_e, out_o, held, held_o, in_sem, out_sem):
    arriving = [
        pltpu.make_async_copy(elastic.at[v], held.at[v], in_sem.at[v]) for v in range(NV)
    ]
    arriving.append(pltpu.make_async_copy(ocean, held_o, in_sem.at[NV]))
    leaving = [
        pltpu.make_async_copy(held.at[v], out_e.at[v], out_sem.at[v]) for v in range(NV)
    ]
    leaving.append(pltpu.make_async_copy(held_o, out_o, out_sem.at[NV]))
    for copy in arriving:
        copy.start()
    for first, second in zip(arriving, leaving):
        first.wait()
        second.start()
    for copy in leaving:
        copy.wait()


def lane_blocks(indices):
    rows, columns = indices.shape
    return jnp.transpose(indices.reshape(rows, columns // 128, 128), (1, 0, 2))


def body(
    elastic,
    jacobian,
    star_mats,
    stiffness,
    face_proj,
    face_lift,
    clusters,
    neighbours,
    send_faces,
    fault_faces,
    fault_strength,
    seafloor_faces,
    seafloor_slots,
    arrival_cells,
    ocean_state,
    ocean_kernels,
    shallow_mats,
    edge_proj,
    edge_lift,
    ocean_send,
    ocean_neighbours,
):
    anywhere = pl.BlockSpec(memory_space=pl.ANY)
    dma = pltpu.SemaphoreType.DMA
    I32 = jnp.int32
    inputs = (
        elastic,
        jacobian,
        jnp.transpose(star_mats, (1, 0, 2)),
        stiffness,
        jnp.transpose(face_proj, (1, 0, 2)),
        jnp.transpose(face_lift, (2, 0, 1)),
        clusters.reshape(1, E),
        lane_blocks(neighbours).reshape(-1),
        lane_blocks(send_faces).reshape(-1),
        fault_faces.reshape(1, 128),
        fault_strength.reshape(1, 128),
        seafloor_faces,
        seafloor_slots.reshape(1, 512),
        arrival_cells.reshape(8, 128),
        ocean_state,
        jnp.transpose(ocean_kernels, (1, 0, 2)),
        jnp.transpose(shallow_mats, (1, 0, 2)),
        jnp.transpose(edge_proj, (1, 0, 2)),
        jnp.transpose(edge_lift, (2, 0, 1)),
        ocean_send,
        lane_blocks(ocean_neighbours),
        fault_faces,
    )
    results = pl.pallas_call(
        main_kernel,
        out_shape=(
            jax.ShapeDtypeStruct(elastic.shape, BF16),
            jax.ShapeDtypeStruct(ocean_state.shape, F32),
        ),
        in_specs=[anywhere] * len(inputs),
        out_specs=(anywhere, anywhere),
        scratch_shapes=[
            pltpu.VMEM((NV, NB, E), BF16),
            pltpu.VMEM((3, E), F32),
            pltpu.VMEM((NV, 3, NV), F32),
            pltpu.VMEM((3, NB, NB), BF16),
            pltpu.VMEM((NF, 4, NB), BF16),
            pltpu.VMEM((NF, 4, NB), BF16),
            pltpu.VMEM((1, E), I32),
            pltpu.SMEM((4 * E,), I32),
            pltpu.SMEM((2 * BF,), I32),
            pltpu.VMEM((1, 128), I32),
            pltpu.SMEM((128,), I32),
            pltpu.VMEM((1, 128), F32),
            pltpu.SMEM((512,), I32),
            pltpu.VMEM((1, 512), I32),
            pltpu.VMEM((8, 128), I32),
            pltpu.VMEM((NO, NF, OC), F32),
            pltpu.VMEM((NF, 2, NF), F32),
            pltpu.VMEM((NO, 2, NO), F32),
            pltpu.VMEM((NE, 3, NF), F32),
            pltpu.VMEM((NE, 3, NF), F32),
            pltpu.SMEM((2, OBF), I32),
            pltpu.SMEM((OC // 128, 3, 128), I32),
            dma((22,)),
            pltpu.VMEM((ROWS, E), F32),
            pltpu.VMEM((4 * ROWS, E), BF16),
            pltpu.VMEM((ROWS, 4 * ROWS), BF16),
            pltpu.VMEM((ROWS, 8 * MAIN), BF16),
            pltpu.VMEM((ROWS, 5 * MAIN), BF16),
            pltpu.VMEM((ROWS, E), F32),
            pltpu.VMEM((2 * REST, MAIN), F32),
            pltpu.VMEM((E, 5 * MAIN), BF16),
            pltpu.VMEM((128, MAIN), F32),
            pltpu.VMEM((128, MAIN), F32),
            pltpu.VMEM((2, 2, BF, MAIN), BF16),
            pltpu.VMEM((2, 2, BF, MAIN), BF16),
            pltpu.VMEM((NV, NB, E), BF16),
            pltpu.VMEM((NO, NF, OC), F32),
            pltpu.VMEM((48, OC), F32),
            pltpu.VMEM((3 * OC + 2 * OBF + 2 * LEAD, 128), F32),
            pltpu.VMEM((3 * OC, 128), F32),
            pltpu.VMEM((2, OBF, 128), F32),
            pltpu.VMEM((2, OBF, 128), F32),
            pltpu.VMEM((48, OC), F32),
            pltpu.VMEM((512, 128), F32),
            pltpu.VMEM((128, 128), F32),
            pltpu.VMEM((N_DOM, 2, 128), F32),
            pltpu.VMEM((N_DOM, 2, 128), F32),
            pltpu.VMEM((N_SUB, 16, OC), F32),
            dma((2,)),
            dma((2,)),
            dma((2,)),
            dma((2,)),
            dma,
            dma,
            dma((3,)),
            dma((3,)),
            dma((E // CHUNK + 1,)),
        ],
        compiler_params=pltpu.CompilerParams(
            collective_id=0,
            has_side_effects=True,
            vmem_limit_bytes=60 * 1024 * 1024,
        ),
    )(*inputs)
    return pl.pallas_call(
        place_kernel,
        out_shape=(
            jax.ShapeDtypeStruct(elastic.shape, BF16),
            jax.ShapeDtypeStruct(ocean_state.shape, F32),
        ),
        in_specs=[anywhere] * 2,
        out_specs=(anywhere, anywhere),
        scratch_shapes=[
            pltpu.VMEM((NV, NB, E), BF16),
            pltpu.VMEM((NO, NF, OC), F32),
            dma((NV + 1,)),
            dma((NV + 1,)),
        ],
        compiler_params=pltpu.CompilerParams(vmem_limit_bytes=60 * 1024 * 1024),
    )(*results)


def solution(mesh):
    both = ("dom", "sub")
    return jax.shard_map(
        body,
        mesh=mesh,
        in_specs=(
            P(None, None, both),
            P(None, both),
            P(),
            P(),
            P(),
            P(),
            P(both),
            P(None, both),
            P(None, both),
            P(both),
            P(both),
            P(both),
            P(both),
            P(both),
            P(None, None, "dom"),
            P(),
            P(),
            P(),
            P(),
            P(None, "dom"),
            P(None, "dom"),
        ),
        out_specs=(P(None, None, both), P(None, None, "dom")),
        check_vma=False,
    )
```

time: 40.3 us -> 33.8 us (0.84)
  local copies, waits for them, and re-layouts: 5.59 us -> 0 us
  Pallas kernels: 33.6 us -> 32.5 us
    unnamed x49 -> x0, local copies, waits for them, and re-layouts: 5.59 us -> none
    pallas_call x1 -> x2, Pallas kernels: 33.6 us -> 32.5 us  [the longest x1 30.5 us: body(): pl.pallas_call(main_kernel, out_shape=(jax.ShapeDtypeStruct(elastic.shape...]
where the time goes in v1:
time: 33.8 us; the launch traced here: 33.2 us
  Pallas kernels  32.5 us (96%)
  between operations  0.65 us (2%)
    pallas_call x1, Pallas kernels, body(): pl.pallas_call(main_kernel, out_shape=(jax.ShapeDtypeStruct(elastic.shape...  30.5 us
    pallas_call x1, Pallas kernels, body(): pl.pallas_call(place_kernel, out_shape=(jax.ShapeDtypeStruct(elastic.shap...  2.02 us

profile of v1, /device:TPU:0, one launch (start us, length us, event | category | flops | bytes accessed | tf_op | source)
XLA Modules:
  0.0 33.2 jit_solution(10623911083007300805)
XLA Ops:
  0.6 30.5 %shard_map.212 = (bf16[9,35,1024]{2,1,0:T(8,128)(2,1)}, f32[3,15,256]{2,1,0:T(8,128)}) custom-call(bf16[9,35,1024]{2,1,0:T(8,128)(2,1)} %elastic_h.1, f32[3,1024]{1,0:T(4,128)} %jac_h.1, f32[9,3,9]{2,1,0:T(4,128)} %bitcast.25, bf16[3,35,35]{2,1,0:T(8,128)(2,1)} %stiff_h.1, bf16[15,4,35]{2,1,0:T(4,128)(2,1)} %bitcast.27, bf16[15,4,35]{2,1,0:T(4,128)(2,1)} %bitcast.28, ...), custom_call_target="tpu_custom_call" | custom-call | tf_op jit(solution)/shard_map/pallas_call | solution.py:730
  31.1 2.0 %shard_map.213 = (bf16[9,35,1024]{2,1,0:T(8,128)(2,1)}, f32[3,15,256]{2,1,0:T(8,128)}) custom-call(bf16[9,35,1024]{2,1,0:T(8,128)(2,1)} %get-tuple-element.4.elastic, f32[3,15,256]{2,1,0:T(8,128)} %get-tuple-element.5.ocean), custom_call_target="tpu_custom_call" | custom-call | tf_op jit(solution)/shard_map/pallas_call | solution.py:803

commit v2 on v1

--- a/solution.py
+++ b/solution.py
@@ -9,11 +9,11 @@
 
 MESH = pl.DeviceIdType.MESH
 F32, BF16 = jnp.float32, jnp.bfloat16
-HIGHEST = lax.Precision.HIGHEST
 
 NV, NB, NF = 9, 35, 15
 NO, NE = 3, 5
 ROWS = 320
+WIDE = 384
 E = 1024
 BF = 256
 OC, OBF = 256, 32
@@ -54,27 +54,22 @@
     return jnp.where(cond, 1.0, 0.0).astype(dtype)
 
 
-def dot(a, b, precision=None):
+def dot(a, b):
     return lax.dot_general(
-        a, b, (((1,), (0,)), ((), ())), precision=precision, preferred_element_type=F32
+        a.astype(BF16), b.astype(BF16), (((1,), (0,)), ((), ())), preferred_element_type=F32
     )
 
 
-def dot_tn(a, b, precision=None):
+def dot_tn(a, b):
     return lax.dot_general(
-        a, b, (((0,), (0,)), ((), ())), precision=precision, preferred_element_type=F32
+        a.astype(BF16), b.astype(BF16), (((0,), (0,)), ((), ())), preferred_element_type=F32
     )
 
 
-def dot_nt(a, b, precision=None):
+def dot_nt(a, b):
     return lax.dot_general(
-        a, b, (((1,), (1,)), ((), ())), precision=precision, preferred_element_type=F32
+        a.astype(BF16), b.astype(BF16), (((1,), (1,)), ((), ())), preferred_element_type=F32
     )
-
-
-def split(x):
-    high = x.astype(BF16)
-    return high, (x - high.astype(F32)).astype(BF16)
 
 
 def combine(mats, pairs):
@@ -143,6 +138,7 @@
     osend_s,
     onbr_s,
     in_sem,
+    step,
     xf,
     xs,
     wmat,
@@ -266,7 +262,7 @@
     xf[NV * NB :, :] = jnp.zeros((ROWS - NV * NB, E), F32)
     loads["jac"].wait()
     loads["clusters"].wait()
-    step = 0.5 * jnp.exp2(-clusters[...].astype(F32))
+    step[...] = 0.5 * jnp.exp2(-clusters[...].astype(F32))
     chunks = [slice(c * CHUNK, (c + 1) * CHUNK) for c in range(E // CHUNK)]
 
     def scaled(x, cols):
@@ -316,11 +312,10 @@
     sublane = iota((8, 128), 0)
 
     def rows8(table, slots8, start=LEAD):
-        taken = table[pl.ds(slots8[0] + start, 8), :]
-        for k in range(1, 8):
-            taken = jnp.where(
-                sublane == k, table[pl.ds(slots8[k] + (start - k), 8), :], taken
-            )
+        taken = None
+        for k in range(8):
+            row = jnp.broadcast_to(table[pl.ds(slots8[k] + start, 1), :], (8, 128))
+            taken = row if k == 0 else jnp.where(sublane == k, row, taken)
         return taken
 
     loads["floor"].wait()
@@ -373,13 +368,31 @@
             first = pl.multiple_of(i * 16, 16)
             for side in range(2):
                 slots = [send_s[part_ * 256 + side * 128 + first + n] for n in range(16)]
-                for half, start in enumerate((LEAD, LEAD + REST)):
-                    taken = [rows8(ext, slots[8 * h : 8 * h + 8], start) for h in range(2)]
-                    rows = pl.ds(part_ * 128 + first, 16)
-                    fsend[side, half, rows, :] = jnp.concatenate(taken, axis=0).astype(BF16)
+                taken = [rows8(ext, slots[8 * h : 8 * h + 8]) for h in range(2)]
+                rows = pl.ds(part_ * 128 + first, 16)
+                fsend[side, rows, :] = jnp.concatenate(taken, axis=0).astype(BF16)
             return carry
 
         lax.fori_loop(0, 128 // 16, gather_send, 0)
+    face_lane = lax.shift_right_logical(iota((8, 128), 1), 5)
+
+    def gather_send_rest(i, carry):
+        first = pl.multiple_of(i * 16, 16)
+        for side in range(2):
+            packed = []
+            for h in range(2):
+                whole = None
+                for g in range(4):
+                    at = (g // 2) * 256 + side * 128 + (g % 2) * 64 + 8 * h
+                    slots8 = [send_s[first + (at + n)] for n in range(8)]
+                    taken = rows8(ext, slots8, LEAD + REST)
+                    whole = taken if g == 0 else jnp.where(face_lane == g, taken, whole)
+                packed.append(whole)
+            rows = pl.ds(BF + first, 16)
+            fsend[side, rows, :] = jnp.concatenate(packed, axis=0).astype(BF16)
+        return carry
+
+    lax.fori_loop(0, 64 // 16, gather_send_rest, 0)
     face_copies = []
     for side, there in ((0, before_id), (1, after_id)):
         copy = pltpu.make_async_remote_copy(
@@ -411,9 +424,9 @@
     ost[NO * NF :, :] = jnp.zeros((48 - NO * NF, OC), F32)
     eprojs = [eproj[:, g, :] for g in range(3)]
     for g in range(3):
-        proj = dot(opick_b, dot_tn(eprojs[g], osel_k, HIGHEST), HIGHEST)
+        proj = dot(opick_b, dot_tn(eprojs[g], osel_k))
         proj = jnp.where((orow_v == o_u) & o_ok, proj, 0.0)
-        oext[LEAD + g * OC : LEAD + (g + 1) * OC, :] = dot_tn(ost[...], proj, HIGHEST)
+        oext[LEAD + g * OC : LEAD + (g + 1) * OC, :] = dot_tn(ost[...], proj)
     for side in range(2):
         for j in range(OBF):
             osend[side, j : j + 1, :] = oext[pl.ds(osend_s[side, j] + LEAD, 1), :]
@@ -434,30 +447,36 @@
     flifts = flift[...].astype(F32)
     flifts = [flifts[:, f, :].astype(BF16) for f in range(4)]
     eye = onehot(iota((NV, NV), 0) == iota((NV, NV), 1), F32)
-    sel_u = [onehot((h_u == iota((NV, MAIN), 0)) & h_ok) for h_u, h_j, h_ok in halves]
-    sel_u = jnp.concatenate(sel_u, axis=1)
-    sel_jj = jnp.concatenate(sel_j, axis=1)
+    last = iota((1, WIDE), 1)
+    last_u = div35(last)
+    last_c = last - NB * last_u
+    wide_u = onehot(last_u == iota((NV, WIDE), 0))
+    wide_c = onehot(last_c == iota((NB, WIDE), 0))
+    down = iota((2 * MAIN, 1), 0)
+    down_lane = down & (MAIN - 1)
+    down_r = down_lane & 31
+    down_q = jnp.where(down < MAIN, down_lane, MAIN + down_r)
+    down_u, down_j, down_ok = face_columns(down_q)
+    down_ok = down_ok & ((down < MAIN) | (down_r < 8))
+    down_u = onehot((down_u == iota((2 * MAIN, NV), 1)) & down_ok)
+    down_j = onehot((down_j == iota((2 * MAIN, NF), 1)) & down_ok)
+    down_face = lax.shift_right_logical(down_lane[MAIN:], 5)
     own = [None, None, None]
-    mrest = jnp.zeros((ROWS, MAIN), F32)
+    mrest = jnp.zeros((MAIN, WIDE), F32)
     for f in range(4):
         normal = 0.5 * (eye - combine(stars, TET[f]))
-        both = spread(pick_v, normal, sel_u) * dot(
-            pick_b, dot_tn(flifts[f], sel_jj).astype(BF16)
+        both = dot(down_u, dot_tn(normal, wide_u)) * dot(
+            down_j, dot(flifts[f], wide_c)
         )
-        mmat[:, f * MAIN : (f + 1) * MAIN] = both[:, :MAIN].astype(BF16)
-        mrest = mrest + jnp.where(
-            lax.shift_right_logical(lane, 5) == f, both[:, MAIN:], 0.0
-        )
+        mmat[f * MAIN : (f + 1) * MAIN, :] = both[:MAIN].astype(BF16)
+        mrest = mrest + jnp.where(down_face == f, both[MAIN:], 0.0)
         through = dot_tn(flifts[f], fprojs[f])
         for d, factor in TET[f]:
             term = through * -factor
             own[d] = term if own[d] is None else own[d] + term
-    mmat[:, 4 * MAIN :] = mrest.astype(BF16)
-    last = iota((1, ROWS), 1)
-    last_u = div35(last)
-    last_c = last - NB * last_u
-    sel_u4 = onehot(last_u == iota((NV, ROWS), 0))
-    sel_c4 = onehot(last_c == iota((NB, ROWS), 0))
+    mmat[4 * MAIN : 5 * MAIN, :] = mrest.astype(BF16)
+    sel_u4 = wide_u[:, :ROWS]
+    sel_c4 = wide_c[:, :ROWS]
     total = jnp.zeros((ROWS, ROWS), F32)
     for d in range(3):
         total = total + spread(pick_v, stars[d], sel_u4) * spread(pick_b, own[d], sel_c4)
@@ -466,6 +485,93 @@
         scaled(xs[3 * ROWS :, cols].astype(F32), cols)
     for cols in chunks:
         accf[:, cols] = xf[:, cols] + dot(wmat[...], xs[:, cols])
+
+    loads["onbr"].wait()
+    loads["okern"].wait()
+    loads["shal"].wait()
+    loads["elift"].wait()
+    for side in range(2):
+        ocean_copies[side].wait_recv()
+    first = LEAD + 3 * OC
+    oext[first : first + OBF, :] = orecv[0] * (dom > 0).astype(F32)
+    oext[first + OBF : first + 2 * OBF, :] = orecv[1] * (dom < N_DOM - 1).astype(F32)
+
+    for part_ in range(OC // 128):
+
+        def ocean_gather(i, carry):
+            for g in range(3):
+                slots8 = [onbr_s[part_, g, i * 8 + n] for n in range(8)]
+                rows = pl.ds(pl.multiple_of(g * OC + part_ * 128 + i * 8, 8), 8)
+                obeside[rows, :] = rows8(oext, slots8)
+            return carry
+
+        lax.fori_loop(0, 128 // 8, ocean_gather, 0)
+    shals = [shal[:, d, :] for d in range(2)]
+    elifts = [elift[:, g, :] for g in range(3)]
+    oeye = onehot(iota((NO, NO), 0) == iota((NO, NO), 1), F32)
+    inner = [okern[:, d, :] for d in range(2)]
+    updated = ost[...]
+    for g in range(3):
+        through = dot_tn(elifts[g], eprojs[g])
+        for d, factor in TRI[g]:
+            inner[d] = inner[d] - factor * through
+        normal = 0.25 * (oeye - combine(shals, TRI[g]))
+        outer = dot(opick_v, dot(normal, osel_u))
+        lifts = dot(opick_b, dot_tn(elifts[g], osel_k))
+        ojump = obeside[g * OC : (g + 1) * OC, :] - oext[LEAD + g * OC : LEAD + (g + 1) * OC, :]
+        updated = updated + dot_nt(outer * lifts, ojump)
+    volume = jnp.zeros((48, 48), F32)
+    for d in range(2):
+        left = dot_nt(dot(opick_v, shals[d]), opick_v)
+        right = dot_nt(dot(opick_b, inner[d]), opick_b)
+        volume = volume + left * right
+    oacc[...] = updated + 0.5 * dot(volume, ost[...])
+
+    for copy in face_copies:
+        copy.wait_recv()
+    has_before = (block > 0).astype(F32)
+    has_after = (block < n_blocks - 1).astype(F32)
+    for side, keep in ((0, has_before), (1, has_after)):
+        first = LEAD + 4 * E + side * BF
+        ext[first : first + BF, :] = frecv[side, :BF, :].astype(F32) * keep
+        packed = frecv[side, BF:, :].astype(F32) * keep
+        for g in range(4):
+            one = jnp.where(lax.shift_right_logical(lane, 5) == g, packed, 0.0)
+            one = one + pltpu.roll(one, 32, 1)
+            one = one + pltpu.roll(one, 64, 1)
+            ext[REST + first + 64 * g : REST + first + 64 * (g + 1), :] = one
+
+    loads["nbr_s"].wait()
+
+    def gather_block(block8, carry):
+        def gather(i, carry):
+            rests = []
+            mains = [[], [], [], []]
+            near_first = block8 * 512 + i * 16
+            for h in range(2):
+                e = pl.multiple_of(block8 * 128 + i * 16 + 8 * h, 8)
+                rest = None
+                for f in range(4):
+                    slots8 = [nbr_s[near_first + (f * 128 + 8 * h + n)] for n in range(8)]
+                    own_row = LEAD + f * E + e
+                    mains[f].append(
+                        rows8(ext, slots8) - ext[pl.ds(pl.multiple_of(own_row, 8), 8), :]
+                    )
+                    own_row = pl.multiple_of(own_row + REST, 8)
+                    jump = rows8(ext, slots8, LEAD + REST) - ext[pl.ds(own_row, 8), :]
+                    rest = jump if f == 0 else jnp.where(face_lane == f, jump, rest)
+                rests.append(rest)
+            rows = pl.ds(pl.multiple_of(block8 * 128 + i * 16, 16), 16)
+            for f in range(4):
+                jm[rows, f * MAIN : (f + 1) * MAIN] = jnp.concatenate(
+                    mains[f], axis=0
+                ).astype(BF16)
+            jm[rows, 4 * MAIN : 5 * MAIN] = jnp.concatenate(rests, axis=0).astype(BF16)
+            return carry
+
+        return lax.fori_loop(0, 128 // 16, gather, carry)
+
+    lax.fori_loop(0, 1, gather_block, 0)
 
     loads["arrival"].wait()
     wide = iota((1, 1024), 1)
@@ -491,7 +597,7 @@
             lax.shift_right_logical(lane, 4) == p, dot(hits, arrived), 0.0
         )
     fold = onehot((lane & 15) == iota((16, 128), 0), F32)
-    part[sub] = dot_nt(fold, forced, HIGHEST)
+    part[sub] = dot_nt(fold, forced)
     part_copies = []
     for k in range(1, N_SUB):
         copy = pltpu.make_async_remote_copy(
@@ -505,47 +611,7 @@
         copy.start()
         part_copies.append(copy)
 
-    for copy in face_copies:
-        copy.wait_recv()
-    has_before = (block > 0).astype(F32)
-    has_after = (block < n_blocks - 1).astype(F32)
-    for half in range(2):
-        first = half * REST + LEAD + 4 * E
-        ext[first : first + BF, :] = frecv[0, half].astype(F32) * has_before
-        ext[first + BF : first + 2 * BF, :] = frecv[1, half].astype(F32) * has_after
-
-    loads["nbr_s"].wait()
-    face_lane = lax.shift_right_logical(iota((8, 128), 1), 5)
-
-    def gather_block(block8, carry):
-        def gather(i, carry):
-            rests = []
-            mains = [[], [], [], []]
-            near_first = block8 * 512 + i * 16
-            for h in range(2):
-                e = pl.multiple_of(block8 * 128 + i * 16 + 8 * h, 8)
-                rest = None
-                for f in range(4):
-                    slots8 = [nbr_s[near_first + (f * 128 + 8 * h + n)] for n in range(8)]
-                    own_row = LEAD + f * E + e
-                    mains[f].append(
-                        rows8(ext, slots8) - ext[pl.ds(pl.multiple_of(own_row, 8), 8), :]
-                    )
-                    own_row = pl.multiple_of(own_row + REST, 8)
-                    jump = rows8(ext, slots8, LEAD + REST) - ext[pl.ds(own_row, 8), :]
-                    rest = jump if f == 0 else jnp.where(face_lane == f, jump, rest)
-                rests.append(rest)
-            rows = pl.ds(pl.multiple_of(block8 * 128 + i * 16, 16), 16)
-            for f in range(4):
-                jm[rows, f * MAIN : (f + 1) * MAIN] = jnp.concatenate(
-                    mains[f], axis=0
-                ).astype(BF16)
-            jm[rows, 4 * MAIN :] = jnp.concatenate(rests, axis=0).astype(BF16)
-            return carry
-
-        return lax.fori_loop(0, 128 // 16, gather, carry)
-
-    lax.fori_loop(0, E // 128, gather_block, 0)
+    lax.fori_loop(1, E // 128, gather_block, 0)
 
     loads["fault"].wait()
     loads["fault_s"].wait()
@@ -580,68 +646,26 @@
         jnp.where(fault_face == lax.shift_right_logical(lane, 5), change_rest, 0.0)
     )
     changes = jnp.concatenate(changes, axis=1).astype(BF16)
-    lifted = dot_nt(mmat[...], changes).astype(BF16)
-    fault_elem = (faults & (E - 1))[:, :1]
-
+    mmat[5 * MAIN :, :] = dot(changes, mmat[: 5 * MAIN, :]).astype(BF16)
+    fault_elem = fault[...] & (E - 1)
+    jm[:, 5 * MAIN :] = onehot(fault_elem == iota((E, 1), 0))
+
+    for cols in chunks:
+        change = jnp.transpose(dot(jm[cols, :], mmat[...]))
+        accf[:, cols] = accf[:, cols] + change[:ROWS]
     out_copies = []
-    for c, cols in enumerate(chunks):
-        at = onehot(fault_elem == iota((1, CHUNK), 1) + c * CHUNK)
-        accf[:, cols] = accf[:, cols] + dot_nt(mmat[...], jm[cols, :]) + dot(lifted, at)
-        for v in range(NV):
-            out_e[v, :, cols] = accf[NB * v : NB * (v + 1), cols].astype(BF16)
-        copy = pltpu.make_async_copy(
-            out_e.at[:, :, cols], out_e_h.at[:, :, cols], out_sem.at[c]
-        )
+    for v in range(NV):
+        out_e[v] = accf[NB * v : NB * (v + 1), :].astype(BF16)
+        copy = pltpu.make_async_copy(out_e.at[v], out_e_h.at[v], out_sem.at[v])
         copy.start()
         out_copies.append(copy)
-
-    loads["onbr"].wait()
-    loads["okern"].wait()
-    loads["shal"].wait()
-    loads["elift"].wait()
-    for side in range(2):
-        ocean_copies[side].wait_recv()
-    first = LEAD + 3 * OC
-    oext[first : first + OBF, :] = orecv[0] * (dom > 0).astype(F32)
-    oext[first + OBF : first + 2 * OBF, :] = orecv[1] * (dom < N_DOM - 1).astype(F32)
-
-    for part_ in range(OC // 128):
-
-        def ocean_gather(i, carry):
-            for g in range(3):
-                slots8 = [onbr_s[part_, g, i * 8 + n] for n in range(8)]
-                rows = pl.ds(pl.multiple_of(g * OC + part_ * 128 + i * 8, 8), 8)
-                obeside[rows, :] = rows8(oext, slots8)
-            return carry
-
-        lax.fori_loop(0, 128 // 8, ocean_gather, 0)
-    shals = [shal[:, d, :] for d in range(2)]
-    elifts = [elift[:, g, :] for g in range(3)]
-    oeye = onehot(iota((NO, NO), 0) == iota((NO, NO), 1), F32)
-    inner = [okern[:, d, :] for d in range(2)]
-    updated = ost[...]
-    for g in range(3):
-        through = dot_tn(elifts[g], eprojs[g], HIGHEST)
-        for d, factor in TRI[g]:
-            inner[d] = inner[d] - factor * through
-        normal = 0.25 * (oeye - combine(shals, TRI[g]))
-        outer = dot(opick_v, dot(normal, osel_u, HIGHEST), HIGHEST)
-        lifts = dot(opick_b, dot_tn(elifts[g], osel_k, HIGHEST), HIGHEST)
-        ojump = obeside[g * OC : (g + 1) * OC, :] - oext[LEAD + g * OC : LEAD + (g + 1) * OC, :]
-        updated = updated + dot_nt(outer * lifts, ojump, HIGHEST)
-    volume = jnp.zeros((48, 48), F32)
-    for d in range(2):
-        left = dot_nt(dot(opick_v, shals[d], HIGHEST), opick_v, HIGHEST)
-        right = dot_nt(dot(opick_b, inner[d], HIGHEST), opick_b, HIGHEST)
-        volume = volume + left * right
-    oacc[...] = updated + 0.5 * dot(volume, ost[...], HIGHEST)
 
     for copy in part_copies:
         copy.wait_recv()
     oacc[:16, :] = oacc[:16, :] + (part[0] + part[1] + part[2] + part[3])
     for v in range(NO):
         out_o[v] = oacc[NF * v : NF * (v + 1), :]
-    copy = pltpu.make_async_copy(out_o, out_o_h, out_sem.at[E // CHUNK])
+    copy = pltpu.make_async_copy(out_o, out_o_h, out_sem.at[NV])
     copy.start()
     out_copies.append(copy)
 
@@ -759,18 +783,19 @@
             pltpu.SMEM((2, OBF), I32),
             pltpu.SMEM((OC // 128, 3, 128), I32),
             dma((22,)),
+            pltpu.VMEM((1, E), F32),
             pltpu.VMEM((ROWS, E), F32),
             pltpu.VMEM((4 * ROWS, E), BF16),
             pltpu.VMEM((ROWS, 4 * ROWS), BF16),
             pltpu.VMEM((ROWS, 8 * MAIN), BF16),
-            pltpu.VMEM((ROWS, 5 * MAIN), BF16),
+            pltpu.VMEM((6 * MAIN, WIDE), BF16),
             pltpu.VMEM((ROWS, E), F32),
             pltpu.VMEM((2 * REST, MAIN), F32),
-            pltpu.VMEM((E, 5 * MAIN), BF16),
+            pltpu.VMEM((E, 6 * MAIN), BF16),
             pltpu.VMEM((128, MAIN), F32),
             pltpu.VMEM((128, MAIN), F32),
-            pltpu.VMEM((2, 2, BF, MAIN), BF16),
-            pltpu.VMEM((2, 2, BF, MAIN), BF16),
+            pltpu.VMEM((2, BF + 64, MAIN), BF16),
+            pltpu.VMEM((2, BF + 64, MAIN), BF16),
             pltpu.VMEM((NV, NB, E), BF16),
             pltpu.VMEM((NO, NF, OC), F32),
             pltpu.VMEM((48, OC), F32),
@@ -792,7 +817,7 @@
             dma,
             dma((3,)),
             dma((3,)),
-            dma((E // CHUNK + 1,)),
+            dma((NV + 1,)),
         ],
         compiler_params=pltpu.CompilerParams(
             collective_id=0,

time: 33.8 us -> 31.8 us (0.941)
  the two profiles are of different devices: /device:TPU:0 before, /device:TPU:24 now
where the time goes in v2:
time: 31.8 us; the launch traced here: 31.7 us
  Pallas kernels  31 us (97%)
  between operations  0.65 us (2%)
    pallas_call x1, Pallas kernels, body(): pl.pallas_call(main_kernel, out_shape=(jax.ShapeDtypeStruct(elastic.shape...  29 us
    pallas_call x1, Pallas kernels, body(): pl.pallas_call(place_kernel, out_shape=(jax.ShapeDtypeStruct(elastic.shap...  2.02 us

profile of v2, /device:TPU:24, one launch (start us, length us, event | category | flops | bytes accessed | tf_op | source)
XLA Modules:
  0.0 31.7 jit_solution(9123674185841886206)
XLA Ops:
  0.6 29.0 %shard_map.212 = (bf16[9,35,1024]{2,1,0:T(8,128)(2,1)}, f32[3,15,256]{2,1,0:T(8,128)}) custom-call(bf16[9,35,1024]{2,1,0:T(8,128)(2,1)} %elastic_h.1, f32[3,1024]{1,0:T(4,128)} %jac_h.1, f32[9,3,9]{2,1,0:T(4,128)} %bitcast.25, bf16[3,35,35]{2,1,0:T(8,128)(2,1)} %stiff_h.1, bf16[15,4,35]{2,1,0:T(4,128)(2,1)} %bitcast.27, bf16[15,4,35]{2,1,0:T(4,128)(2,1)} %bitcast.28, ...), custom_call_target="tpu_custom_call" | custom-call | tf_op jit(solution)/shard_map/pallas_call | solution.py:754
  29.7 2.0 %shard_map.213 = (bf16[9,35,1024]{2,1,0:T(8,128)(2,1)}, f32[3,15,256]{2,1,0:T(8,128)}) custom-call(bf16[9,35,1024]{2,1,0:T(8,128)(2,1)} %get-tuple-element.4.elastic, f32[3,15,256]{2,1,0:T(8,128)} %get-tuple-element.5.ocean), custom_call_target="tpu_custom_call" | custom-call | tf_op jit(solution)/shard_map/pallas_call | solution.py:828
